TPU v7x, 512 devices: a whole 4x8x8 slice. The times are simulated.
512 devices in a mesh: dom: 32 (over x, z_hi, core), band: 16 (over z_lo, y).
Axes of the slice: x: 4, y: 8, z: 8 (z_hi: 4, z_lo: 2; z = z_hi * 2 + z_lo), core: 2. Of those that a mesh axis runs over, the one named last changes fastest.
Arguments:
- wave_block: float32 [16, 384, 16, 128], P('band', 'dom'), may hold values from -6 to 6
- potential: float32 [384, 16, 128], P('dom'), may hold values from -1.5 to 1
- projectors: float32 [1024, 8, 2048], P('dom', None, 'band'), may hold values from -0.25 to 0.25
- kb_energy: float32 [512, 8], P('dom'), may hold values from 1 to 6
- slot_atom: int32 [1024], P('dom'), may hold values from 0 to 511, as said below
- slot_corner: int32 [3, 1024], P(None, 'dom'), may hold values from 0 to 112, as said below
Outputs:
- filtered: float32 [16, 384, 16, 128], P('band', 'dom')
Inputs may be any that keep to these rules, and one draw needn't show every extreme that they name: `slot_atom`: the slots of slab t are rows t * 32 to (t + 1) * 32 - 1; each names an atom owned by slab t - 1, t or t + 1, where atom a is owned by slab a // 16. `slot_corner`: rows 0, 1, 2 give the box's first cell inside its slab along the three dimensions, at most 4, 0 and 112.
All inputs are finite; a program needn't handle non-finite values.
Results may differ from a plain program's by a relative error of at most 0.00024.
Values sent between devices are 32-bit elements; how exact they have to be, the bound alone decides.
A program may use at most 64 MiB of HBM per device.

v0:
```python
import jax
import jax.numpy as jnp
from jax import lax
from jax.experimental import pallas as pl
from jax.experimental.pallas import tpu as pltpu
from jax.sharding import PartitionSpec as P

SX, SY, SZ, DEGREE, PROJ = 8, 16, 16, 3, 8
CX, CY, CZ = 12, 16, 128
SLOTS, ATOM_DEV = 32, 16
LANES = SLOTS * SZ
ROWS = CX * CY
REACH = 6
Y_RING = 8
PARTS = 4
HALF = PARTS // 2
PROJ_PART = PROJ // PARTS
SENDS = 5 * PARTS
STENCIL = (
    -5369.0 / 1800.0,
    12.0 / 7.0,
    -15.0 / 56.0,
    10.0 / 189.0,
    -1.0 / 112.0,
    2.0 / 1925.0,
    -1.0 / 16632.0,
)
KINETIC = tuple(-0.5 * weight for weight in STENCIL)
LOWER_EDGE, UPPER_EDGE, ANCHOR_POINT = 3.0, 30.0, 0.5
F32, BF16 = jnp.float32, jnp.bfloat16
MESH = pl.DeviceIdType.MESH
REACHED = (1, 2, -1, -2)


def split(x):
    high = x.astype(BF16)
    return high, (x - high.astype(F32)).astype(BF16)


def dot(a, b):
    return jnp.dot(a, b, preferred_element_type=F32)


def iota(shape, dim):
    return lax.broadcasted_iota(jnp.int32, shape, dim)


def weight_at(distance, centre):
    out = jnp.where(distance == 0, F32(centre), F32(0.0))
    for k in range(1, REACH + 1):
        out = jnp.where(distance == k, F32(KINETIC[k]), out)
    return out


def coefficients():
    half_width = (UPPER_EDGE - LOWER_EDGE) / 2.0
    centre = (UPPER_EDGE + LOWER_EDGE) / 2.0
    sigma_first = half_width / (ANCHOR_POINT - centre)
    out = [(sigma_first / half_width, 0.0)]
    sigma = sigma_first
    for _ in range(2, DEGREE + 1):
        following = 1.0 / (2.0 / sigma_first - sigma)
        out.append((2.0 * following / half_width, sigma * following))
        sigma = following
    return centre, out


def transposed_parts(x):
    row, col = iota((8, 128), 0), iota((8, 128), 1) >> 4
    for bit in (1, 2, 4):
        row_bit, col_bit = (row & bit) != 0, (col & bit) != 0
        down = pltpu.roll(pltpu.roll(x, bit, 0), 128 - 16 * bit, 1)
        up = pltpu.roll(pltpu.roll(x, 8 - bit, 0), 16 * bit, 1)
        x = jnp.where(row_bit == col_bit, x, jnp.where(row_bit, down, up))
    return x


def kernel(
    wave_ref, pot_ref, proj_ref, kb_ref, atom_ref, corner_ref, out_ref,
    pbuf, halo, part_own, part_in, kb_own, kb_in, kb_pad, fields, boxes, acc, deposit_in,
    pick_z, pick_zt, pick_atom, pick_atom_t, band_z, cross, x_corner, local,
    gather_out, gather_in, halo_out, halo_in_sem, part_out_sem, part_in_sem, kb_out_sem, kb_in_sem,
):
    dom, band = lax.axis_index("dom"), lax.axis_index("band")
    doms = lax.axis_size("dom")
    y, z = lax.rem(band, Y_RING), lax.div(band, Y_RING)

    def dom_at(step):
        return lax.rem(dom + step + doms, doms)

    def band_at(dy, other):
        column = 1 - z if other else z
        return column * Y_RING + lax.rem(y + dy + Y_RING, Y_RING)

    gather_to = (band_at(1, False), band_at(-1, False), band_at(0, True))

    barrier = pltpu.get_barrier_semaphore()
    for target in gather_to:
        pl.semaphore_signal(barrier, inc=1, device_id=(dom, target), device_id_type=MESH)
    for step in REACHED:
        pl.semaphore_signal(barrier, inc=1, device_id=(dom_at(step), band), device_id_type=MESH)

    for p in range(PROJ):
        for g in range(4):
            x = proj_ref[pl.ds(64 * g + p, 8, stride=8), :]
            pbuf[band, p, :, pl.ds(128 * g, 128)] = transposed_parts(x)
    pad_rows = iota((128, 128), 0)
    kb_pad[...] = jnp.zeros((128, 128), F32)
    kb_pad[0:ATOM_DEV, 0:PROJ] = kb_ref[...]
    kb_own[...] = jnp.transpose(kb_pad[...])[0:8, :]

    pl.semaphore_wait(barrier, 3 + len(REACHED))

    def piece(way, n, owner, part):
        ref = pbuf.at[owner, pl.ds(part * PROJ_PART, PROJ_PART)]
        return pltpu.make_async_remote_copy(
            src_ref=ref, dst_ref=ref, send_sem=gather_out.at[way, n], recv_sem=gather_in.at[way, n],
            device_id=(dom, gather_to[way]), device_id_type=MESH,
        )

    sent = []

    def send(way, n, owner, part):
        copy = piece(way, n, owner, part)
        copy.start()
        sent.append(copy)

    def received(way, n, owner, part):
        piece(way, n, owner, part).wait_recv()

    for part in range(PARTS):
        for way in range(3):
            send(way, part, band, part)

    def halo_copy(app, side, source):
        planes = pl.ds(CX - REACH, REACH) if side == 0 else pl.ds(0, REACH)
        return pltpu.make_async_remote_copy(
            src_ref=source.at[planes], dst_ref=halo.at[app, side],
            send_sem=halo_out.at[app, side], recv_sem=halo_in_sem.at[app, side],
            device_id=(dom_at(1 if side == 0 else -1), band), device_id_type=MESH,
        )

    def part_copy(app, n):
        return pltpu.make_async_remote_copy(
            src_ref=part_own.at[app], dst_ref=part_in.at[app, n],
            send_sem=part_out_sem.at[app, n], recv_sem=part_in_sem.at[app, n],
            device_id=(dom_at(REACHED[n]), band), device_id_type=MESH,
        )

    def kb_copy(n):
        return pltpu.make_async_remote_copy(
            src_ref=kb_own, dst_ref=kb_in.at[n], send_sem=kb_out_sem.at[n], recv_sem=kb_in_sem.at[n],
            device_id=(dom_at(1 if n == 0 else -1), band), device_id_type=MESH,
        )

    def field(app):
        return wave_ref.at[0] if app == 0 else fields.at[app - 1]

    for n in range(2):
        kb_copy(n).start()
    for side in range(2):
        halo_copy(0, side, field(0)).start()

    lane = iota((8, 128), 1)
    lane_slot, lane_cell = lane >> 4, lane & 15
    first_atom = (dom - 1) * ATOM_DEV
    for g in range(4):
        at_x, at_z, atom = (jnp.zeros((8, 128), jnp.int32) for _ in range(3))
        for q in range(8):
            here = lane_slot == q
            at_x = jnp.where(here, corner_ref[0, 8 * g + q], at_x)
            at_z = jnp.where(here, corner_ref[2, 8 * g + q], at_z)
            atom = jnp.where(here, atom_ref[8 * g + q] - first_atom, atom)
        lanes = pl.ds(128 * g, 128)
        x_corner[:, lanes] = at_x
        hot_z = jnp.where(pad_rows == (at_z + lane_cell)[0:1, :], F32(1.0), F32(0.0))
        pick_z[:, lanes] = hot_z.astype(BF16)
        pick_zt[lanes, :] = jnp.transpose(hot_z).astype(BF16)
        hot_atom = jnp.where(pad_rows == atom[0:1, :], F32(1.0), F32(0.0))
        pick_atom[:, lanes] = hot_atom.astype(BF16)
        pick_atom_t[lanes, :] = jnp.transpose(hot_atom).astype(BF16)

    def extract(app):
        rows = field(app)[...].reshape(ROWS, CZ)
        high, low = split(rows)
        for g in range(4):
            lanes = pl.ds(128 * g, 128)
            hot = pick_z[:, lanes]
            along_z = (dot(high, hot) + dot(low, hot)).reshape(CX, CY, 128)
            at_x = x_corner[:, lanes][None, 0:1, :]
            cut = along_z[0:SX]
            for d in range(1, CX - SX + 1):
                cut = jnp.where(at_x == d, along_z[d : d + SX], cut)
            boxes[:, :, lanes] = cut.reshape(2 * SX, 8, 128)

    extract(0)

    distance = jnp.abs(iota((CZ, CZ), 0) - iota((CZ, CZ), 1))
    band_z[:, 0:128], band_z[:, 128:256] = split(weight_at(distance, 3.0 * KINETIC[0]))
    row, col = iota((ROWS, ROWS), 0), iota((ROWS, ROWS), 1)
    gap_x, gap_y = jnp.abs((row >> 4) - (col >> 4)), jnp.abs((row & 15) - (col & 15))
    gap = jnp.where(gap_x == 0, gap_y, jnp.where(gap_y == 0, gap_x, 99))
    cross[0:ROWS, :], cross[ROWS:, :] = split(weight_at(gap, 0.0))
    acc[...] = jnp.zeros((PROJ, 8, LANES), F32)

    def accumulate(owner, part):
        here = pl.ds(part * PROJ_PART, PROJ_PART)
        acc[here] = acc[here] + pbuf[owner, here] * boxes[owner][None]

    def apply_local(app):
        rows = field(app)[...].reshape(ROWS, CZ)
        high, low = split(rows)
        weights = band_z[...]
        both = dot(high, weights)
        out = both[:, 0:128] + both[:, 128:256] + dot(low, weights[:, 0:128])
        both = dot(cross[...], jnp.concatenate([high, low], axis=1))
        out = out + (both[0:ROWS, 0:128] + both[0:ROWS, 128:256] + both[ROWS:, 0:128])
        out = out + pot_ref[...].reshape(ROWS, CZ) * rows
        local[...] = out.reshape(CX, CY, CZ)

    def add_halo(app):
        for side in range(2):
            halo_copy(app, side, field(app)).wait_recv()
        low = jnp.where(dom > 0, halo[app, 0], F32(0.0))
        high = jnp.where(dom < doms - 1, halo[app, 1], F32(0.0))
        for x in range(REACH):
            local[x] = local[x] + sum(F32(KINETIC[k]) * low[REACH + x - k] for k in range(x + 1, REACH + 1))
            at = CX - 1 - x
            local[at] = local[at] + sum(F32(KINETIC[k]) * high[k - 1 - x] for k in range(x + 1, REACH + 1))

    both_halves = tuple(range(PARTS))
    first_half, last_half = both_halves[:HALF], both_halves[HALF:]

    for part in both_halves:
        accumulate(band, part)
    z_next = PARTS
    z_expected = [(band_at(0, True), part) for part in both_halves]
    for step in range(1, 5):
        arrived = []
        for part in both_halves:
            for way, sign in ((0, -1), (1, 1)):
                if step == 4 and part not in (first_half, last_half)[way]:
                    continue
                owner = band_at(sign * step, False)
                n = (step - 1) * PARTS + (part if step < 4 or way == 0 else part - HALF)
                received(way, n, owner, part)
                if step < 3:
                    send(way, step * PARTS + part, owner, part)
                elif step == 3 and part in (first_half, last_half)[way]:
                    send(way, 3 * PARTS + part - (0 if way == 0 else HALF), owner, part)
                if part in last_half or step == 4:
                    send(2, z_next, owner, part)
                    z_expected.append((band_at(sign * step, True), part))
                    z_next += 1
                arrived.append((owner, part))
        other_base = 3 * PARTS + HALF
        if step == 1:
            for part in both_halves:
                owner = band_at(0, True)
                received(2, part, owner, part)
                if part in first_half:
                    for way in range(2):
                        send(way, other_base + part, owner, part)
                arrived.append((owner, part))
        else:
            for part in first_half:
                for way, sign in ((0, -1), (1, 1)):
                    owner = band_at(sign * (step - 1), True)
                    n = other_base + (step - 2) * HALF + part
                    received(way, n, owner, part)
                    if step < 4:
                        send(way, n + HALF, owner, part)
                    arrived.append((owner, part))
        for owner, part in arrived:
            accumulate(owner, part)
        if step == 1:
            apply_local(0)
    for n in range(PARTS, SENDS):
        owner, part = z_expected[n]
        received(2, n, owner, part)
        accumulate(owner, part)

    for n in range(2):
        kb_copy(n).wait_recv()
    atom_lane = iota((8, 128), 1)
    energy = jnp.where(
        atom_lane < ATOM_DEV,
        kb_in[0],
        jnp.where(
            atom_lane < 2 * ATOM_DEV,
            pltpu.roll(kb_own[...], ATOM_DEV, 1),
            jnp.where(atom_lane < 3 * ATOM_DEV, pltpu.roll(kb_in[1], 2 * ATOM_DEV, 1), F32(0.0)),
        ),
    )
    centre, coefs = coefficients()
    for app in range(DEGREE):
        if app:
            extract(app)
            for g in range(4):
                lanes = pl.ds(128 * g, 128)
                total = pbuf[0, :, :, lanes] * boxes[0, :, lanes][None]
                for owner in range(1, 2 * SX):
                    total = total + pbuf[owner, :, :, lanes] * boxes[owner, :, lanes][None]
                acc[:, :, lanes] = total
        high, low = split(acc[...].reshape(PROJ * 8, LANES))
        hot = pick_atom_t[...]
        sums = (dot(high, hot) + dot(low, hot)).reshape(PROJ, 8, 128)
        part_own[app] = jnp.sum(sums, axis=1)
        for n in range(len(REACHED)):
            part_copy(app, n).start()
        if app:
            apply_local(app)
        add_halo(app)
        total = part_own[app]
        for n, step in enumerate(REACHED):
            part_copy(app, n).wait_recv()
            inside = (dom - step >= 0) & (dom - step < doms)
            shifted = pltpu.roll(part_in[app, n], (-step * ATOM_DEV) % 128, 1)
            total = total + jnp.where(inside, shifted, F32(0.0))
        high, low = split(total * energy)
        for g in range(4):
            lanes = pl.ds(128 * g, 128)
            hot = pick_atom[:, lanes]
            back = dot(high, hot) + dot(low, hot)
            weights = [jnp.broadcast_to(back[p : p + 1, :], (8, 128)) for p in range(PROJ)]
            at_x = x_corner[:, lanes]
            for half in range(2):
                values = []
                for i in range(SX):
                    value = pbuf[2 * i + half, 0, :, lanes] * weights[0]
                    for p in range(1, PROJ):
                        value = value + pbuf[2 * i + half, p, :, lanes] * weights[p]
                    values.append(value)
                for x in range(CX):
                    spread = jnp.zeros((8, 128), F32)
                    for d in range(max(0, x - SX + 1), min(x, CX - SX) + 1):
                        spread = jnp.where(at_x == d, values[x - d], spread)
                    deposit_in[pl.ds(x * CY + 8 * half, 8), lanes] = spread
        high, low = split(deposit_in[...])
        hot = pick_zt[...]
        nonlocal_part = (dot(high, hot) + dot(low, hot)).reshape(CX, CY, CZ)
        now = field(app)[...]
        scale, keep = coefs[app]
        new = F32(scale) * (local[...] + nonlocal_part - F32(centre) * now)
        if app:
            new = new - F32(keep) * field(app - 1)[...]
        if app < DEGREE - 1:
            fields[app] = new
            for side in range(2):
                halo_copy(app + 1, side, field(app + 1)).start()
        else:
            out_ref[0] = new

    for copy in sent:
        copy.wait_send()
    for n in range(2):
        kb_copy(n).wait_send()
    for app in range(DEGREE):
        for side in range(2):
            halo_copy(app, side, field(app)).wait_send()
        for n in range(len(REACHED)):
            part_copy(app, n).wait_send()


def on_device(wave_block, potential, projectors, kb_energy, slot_atom, slot_corner):
    vmem, smem = pl.BlockSpec(memory_space=pltpu.VMEM), pl.BlockSpec(memory_space=pltpu.SMEM)
    dma = pltpu.SemaphoreType.DMA
    return pl.pallas_call(
        kernel,
        out_shape=jax.ShapeDtypeStruct(wave_block.shape, F32),
        in_specs=[vmem, vmem, vmem, vmem, smem, smem],
        out_specs=vmem,
        scratch_shapes=[
            pltpu.VMEM((2 * SX, PROJ, 8, LANES), F32),
            pltpu.VMEM((DEGREE, 2, REACH, CY, CZ), F32),
            pltpu.VMEM((DEGREE, 8, 128), F32),
            pltpu.VMEM((DEGREE, len(REACHED), 8, 128), F32),
            pltpu.VMEM((8, 128), F32),
            pltpu.VMEM((2, 8, 128), F32),
            pltpu.VMEM((128, 128), F32),
            pltpu.VMEM((DEGREE - 1, CX, CY, CZ), F32),
            pltpu.VMEM((2 * SX, 8, LANES), F32),
            pltpu.VMEM((PROJ, 8, LANES), F32),
            pltpu.VMEM((ROWS, LANES), F32),
            pltpu.VMEM((CZ, LANES), BF16),
            pltpu.VMEM((LANES, CZ), BF16),
            pltpu.VMEM((128, LANES), BF16),
            pltpu.VMEM((LANES, 128), BF16),
            pltpu.VMEM((CZ, 256), BF16),
            pltpu.VMEM((2 * ROWS, ROWS), BF16),
            pltpu.VMEM((8, LANES), jnp.int32),
            pltpu.VMEM((CX, CY, CZ), F32),
            dma((3, SENDS)),
            dma((3, SENDS)),
            dma((DEGREE, 2)),
            dma((DEGREE, 2)),
            dma((DEGREE, len(REACHED))),
            dma((DEGREE, len(REACHED))),
            dma((2,)),
            dma((2,)),
        ],
        compiler_params=pltpu.CompilerParams(
            collective_id=0, has_side_effects=True, vmem_limit_bytes=32 * 1024 * 1024
        ),
        name="chebyshev",
    )(wave_block, potential, projectors.reshape(SLOTS * PROJ, 128), kb_energy, slot_atom, slot_corner)


def solution(mesh):
    placed = (
        P("band", "dom", None, None),
        P("dom", None, None),
        P("dom", None, "band"),
        P("dom", None),
        P("dom"),
        P(None, "dom"),
    )
    return jax.shard_map(
        on_device,
        mesh=mesh,
        in_specs=placed,
        out_specs=P("band", "dom", None, None),
        check_vma=False,
    )
```

profile of v0, /device:TPU:1, one launch (start us, length us, event | category | flops | bytes accessed | tf_op | source)
XLA Modules:
  0.0 57.1 jit_solution(1112755357754962995)
XLA Ops:
  0.0 0.0 copy-start.3
  0.0 0.0 copy-start.4
  0.0 0.8 %copy.7.kb_ref = f32[16,8]{1,0:T(8,128)S(1)} copy(f32[16,8]{0,1:T(8,128)} %param.9) | data formatting | bytes 1024 | tf_op args[3]
  0.8 0.0 copy-done.3
  0.8 0.0 copy-done.4
  0.8 0.0 copy-start
  0.8 0.9 %copy-done = f32[32,8,128]{2,1,0:T(8,128)S(1)} copy-done((f32[32,8,128]{2,1,0:T(8,128)S(1)}, f32[32,8,128]{2,1,0:T(8,128)}, u32[]{:S(2)}) %copy-start) | copy-done | bytes 131096
  1.7 0.0 copy-start.1
  1.7 0.9 %copy-done.1 = f32[1,12,16,128]{3,2,1,0:T(8,128)S(1)} copy-done((f32[1,12,16,128]{3,2,1,0:T(8,128)S(1)}, f32[1,12,16,128]{3,2,1,0:T(8,128)}, u32[]{:S(2)}) %copy-start.1) | copy-done | bytes 98328
  2.6 0.0 copy-start.2
  2.6 0.9 %copy-done.2 = f32[12,16,128]{2,1,0:T(8,128)S(1)} copy-done((f32[12,16,128]{2,1,0:T(8,128)S(1)}, f32[12,16,128]{2,1,0:T(8,128)}, u32[]{:S(2)}) %copy-start.2) | copy-done | bytes 98328
  3.5 53.0 %chebyshev.1 = f32[1,12,16,128]{3,2,1,0:T(8,128)S(1)} custom-call(f32[1,12,16,128]{3,2,1,0:T(8,128)S(1)} %copy-done.1, f32[12,16,128]{2,1,0:T(8,128)S(1)} %copy-done.2, f32[256,128]{1,0:T(8,128)S(1)} %bitcast.1, f32[16,8]{1,0:T(8,128)S(1)} %copy.7.kb_ref, s32[32]{0:T(128)S(1)} %copy-done.4, s32[3,32]{1,0:T(4,128)S(1)} %copy-done.3), custom_call_target="tpu_custom_call" | custom-call | tf_op jit(solution)/shard_map/chebyshev/pallas_call | solution.py:368
  56.5 0.6 %copy.9 = f32[1,12,16,128]{3,2,1,0:T(8,128)} copy(f32[1,12,16,128]{3,2,1,0:T(8,128)S(1)} %chebyshev.1) | data formatting | bytes 196608
Async XLA Ops:
  0.0 0.8 %copy-start.3 = (s32[3,32]{1,0:T(4,128)S(1)}, s32[3,32]{1,0:T(4,128)}, u32[]{:S(2)}) copy-start(s32[3,32]{1,0:T(4,128)} %corner_ref.1) | copy-start | bytes 1156
  0.0 0.8 %copy-start.4 = (s32[32]{0:T(128)S(1)}, s32[32]{0:T(128)}, u32[]{:S(2)}) copy-start(s32[32]{0:T(128)} %atom_ref.1) | copy-start | bytes 388
  0.8 0.9 %copy-start = (f32[32,8,128]{2,1,0:T(8,128)S(1)}, f32[32,8,128]{2,1,0:T(8,128)}, u32[]{:S(2)}) copy-start(f32[32,8,128]{2,1,0:T(8,128)} %param.8) | copy-start | bytes 393220
  1.7 0.9 %copy-start.1 = (f32[1,12,16,128]{3,2,1,0:T(8,128)S(1)}, f32[1,12,16,128]{3,2,1,0:T(8,128)}, u32[]{:S(2)}) copy-start(f32[1,12,16,128]{3,2,1,0:T(8,128)} %wave_ref.1) | copy-start | bytes 294916
  2.6 0.9 %copy-start.2 = (f32[12,16,128]{2,1,0:T(8,128)S(1)}, f32[12,16,128]{2,1,0:T(8,128)}, u32[]{:S(2)}) copy-start(f32[12,16,128]{2,1,0:T(8,128)} %pot_ref.1) | copy-start | bytes 294916
where the time goes:
time: 57.3 us; the launch traced here: 57.1 us
  Pallas kernels  53 us (92%)
  local copies, waits for them, and re-layouts  4.12 us (7%)
    pallas_call x1, Pallas kernels, on_device(): pl.pallas_call(kernel, out_shape=jax.ShapeDtypeStruct(wave_block.shape, F...  53 us
    unnamed x12, local copies, waits for them, and re-layouts  4.12 us

commit v1 on v0

--- a/solution.py
+++ b/solution.py
@@ -76,8 +76,9 @@
 
 
 def kernel(
-    wave_ref, pot_ref, proj_ref, kb_ref, atom_ref, corner_ref, out_ref,
-    pbuf, halo, part_own, part_in, kb_own, kb_in, kb_pad, fields, boxes, acc, deposit_in,
+    wave_hbm, pot_hbm, proj_hbm, kb_hbm, atom_hbm, corner_hbm, out_ref,
+    wave_ref, pot_ref, proj_ref, kb_fetched, atom_ref, corner_ref, fetched,
+    pbuf, halo, part_own, part_in, kb_own, kb_in, fields, boxes, acc, deposit_in,
     pick_z, pick_zt, pick_atom, pick_atom_t, band_z, cross, x_corner, local,
     gather_out, gather_in, halo_out, halo_in_sem, part_out_sem, part_in_sem, kb_out_sem, kb_in_sem,
 ):
@@ -94,22 +95,28 @@
 
     gather_to = (band_at(1, False), band_at(-1, False), band_at(0, True))
 
+    kb_own[...] = jnp.zeros((8, 128), F32)
+    fetches = [
+        pltpu.make_async_copy(source, target, fetched.at[n])
+        for n, (source, target) in enumerate(
+            (
+                (proj_hbm, proj_ref),
+                (wave_hbm.at[0], wave_ref),
+                (corner_hbm, corner_ref),
+                (atom_hbm, atom_ref),
+                (kb_hbm, kb_fetched),
+                (pot_hbm, pot_ref),
+            )
+        )
+    ]
+    for fetch in fetches:
+        fetch.start()
+
     barrier = pltpu.get_barrier_semaphore()
     for target in gather_to:
         pl.semaphore_signal(barrier, inc=1, device_id=(dom, target), device_id_type=MESH)
     for step in REACHED:
         pl.semaphore_signal(barrier, inc=1, device_id=(dom_at(step), band), device_id_type=MESH)
-
-    for p in range(PROJ):
-        for g in range(4):
-            x = proj_ref[pl.ds(64 * g + p, 8, stride=8), :]
-            pbuf[band, p, :, pl.ds(128 * g, 128)] = transposed_parts(x)
-    pad_rows = iota((128, 128), 0)
-    kb_pad[...] = jnp.zeros((128, 128), F32)
-    kb_pad[0:ATOM_DEV, 0:PROJ] = kb_ref[...]
-    kb_own[...] = jnp.transpose(kb_pad[...])[0:8, :]
-
-    pl.semaphore_wait(barrier, 3 + len(REACHED))
 
     def piece(way, n, owner, part):
         ref = pbuf.at[owner, pl.ds(part * PROJ_PART, PROJ_PART)]
@@ -128,7 +135,14 @@
     def received(way, n, owner, part):
         piece(way, n, owner, part).wait_recv()
 
+    fetches[0].wait()
     for part in range(PARTS):
+        for p in range(part * PROJ_PART, (part + 1) * PROJ_PART):
+            for g in range(4):
+                x = proj_ref[pl.ds(64 * g + p, 8, stride=8), :]
+                pbuf[band, p, :, pl.ds(128 * g, 128)] = transposed_parts(x)
+        if part == 0:
+            pl.semaphore_wait(barrier, 3 + len(REACHED))
         for way in range(3):
             send(way, part, band, part)
 
@@ -154,8 +168,11 @@
         )
 
     def field(app):
-        return wave_ref.at[0] if app == 0 else fields.at[app - 1]
-
+        return wave_ref if app == 0 else fields.at[app - 1]
+
+    for fetch in fetches[1:]:
+        fetch.wait()
+    kb_own[:, 0:ATOM_DEV] = kb_fetched[...]
     for n in range(2):
         kb_copy(n).start()
     for side in range(2):
@@ -163,6 +180,7 @@
 
     lane = iota((8, 128), 1)
     lane_slot, lane_cell = lane >> 4, lane & 15
+    pad_rows = iota((128, 128), 0)
     first_atom = (dom - 1) * ATOM_DEV
     for g in range(4):
         at_x, at_z, atom = (jnp.zeros((8, 128), jnp.int32) for _ in range(3))
@@ -363,21 +381,27 @@
 
 
 def on_device(wave_block, potential, projectors, kb_energy, slot_atom, slot_corner):
-    vmem, smem = pl.BlockSpec(memory_space=pltpu.VMEM), pl.BlockSpec(memory_space=pltpu.SMEM)
+    vmem, hbm = pl.BlockSpec(memory_space=pltpu.VMEM), pl.BlockSpec(memory_space=pltpu.HBM)
     dma = pltpu.SemaphoreType.DMA
     return pl.pallas_call(
         kernel,
         out_shape=jax.ShapeDtypeStruct(wave_block.shape, F32),
-        in_specs=[vmem, vmem, vmem, vmem, smem, smem],
+        in_specs=[hbm] * 6,
         out_specs=vmem,
         scratch_shapes=[
+            pltpu.VMEM((CX, CY, CZ), F32),
+            pltpu.VMEM((CX, CY, CZ), F32),
+            pltpu.VMEM((SLOTS * PROJ, 128), F32),
+            pltpu.VMEM((8, ATOM_DEV), F32),
+            pltpu.SMEM((SLOTS,), jnp.int32),
+            pltpu.SMEM((3, SLOTS), jnp.int32),
+            dma((6,)),
             pltpu.VMEM((2 * SX, PROJ, 8, LANES), F32),
             pltpu.VMEM((DEGREE, 2, REACH, CY, CZ), F32),
             pltpu.VMEM((DEGREE, 8, 128), F32),
             pltpu.VMEM((DEGREE, len(REACHED), 8, 128), F32),
             pltpu.VMEM((8, 128), F32),
             pltpu.VMEM((2, 8, 128), F32),
-            pltpu.VMEM((128, 128), F32),
             pltpu.VMEM((DEGREE - 1, CX, CY, CZ), F32),
             pltpu.VMEM((2 * SX, 8, LANES), F32),
             pltpu.VMEM((PROJ, 8, LANES), F32),
@@ -400,10 +424,10 @@
             dma((2,)),
         ],
         compiler_params=pltpu.CompilerParams(
-            collective_id=0, has_side_effects=True, vmem_limit_bytes=32 * 1024 * 1024
+            collective_id=0, has_side_effects=True, vmem_limit_bytes=60 * 1024 * 1024
         ),
         name="chebyshev",
-    )(wave_block, potential, projectors.reshape(SLOTS * PROJ, 128), kb_energy, slot_atom, slot_corner)
+    )(wave_block, potential, projectors.reshape(SLOTS * PROJ, 128), kb_energy.T, slot_atom, slot_corner)
 
 
 def solution(mesh):

time: 57.3 us -> 54.8 us (0.956)
  local copies, waits for them, and re-layouts: 4.12 us -> 1.54 us
    unnamed x12 -> x1, local copies, waits for them, and re-layouts: 4.12 us -> 1.54 us
where the time goes in v1:
time: 54.8 us; the launch traced here: 54.6 us
  Pallas kernels  53.1 us (97%)
  local copies, waits for them, and re-layouts  1.54 us (3%)
    pallas_call x1, Pallas kernels, on_device(): pl.pallas_call(kernel, out_shape=jax.ShapeDtypeStruct(wave_block.shape, F...  53.1 us
    unnamed x1, local copies, waits for them, and re-layouts  1.54 us

profile of v1, /device:TPU:1, one launch (start us, length us, event | category | flops | bytes accessed | tf_op | source)
XLA Modules:
  0.0 54.6 jit_solution(15890599680897401291)
XLA Ops:
  0.0 53.1 %chebyshev.1 = f32[1,12,16,128]{3,2,1,0:T(8,128)} custom-call(f32[1,12,16,128]{3,2,1,0:T(8,128)} %wave_hbm.1, f32[12,16,128]{2,1,0:T(8,128)} %pot_hbm.1, f32[256,128]{1,0:T(8,128)} %bitcast.2, f32[8,16]{1,0:T(8,128)} %bitcast.3, s32[32]{0:T(128)} %atom_hbm.1, s32[3,32]{1,0:T(4,128)} %corner_hbm.1), custom_call_target="tpu_custom_call" | custom-call | tf_op jit(solution)/shard_map/chebyshev/pallas_call | solution.py:386
  53.1 1.5 %copy.8 = f32[1,12,16,128]{3,2,1,0:T(8,128)} copy(f32[1,12,16,128]{3,2,1,0:T(8,128)} %chebyshev.1) | data formatting | bytes 196608

commit v2 on v1

--- a/solution.py
+++ b/solution.py
@@ -1,3 +1,5 @@
+import functools
+
 import jax
 import jax.numpy as jnp
 from jax import lax
@@ -15,7 +17,10 @@
 PARTS = 4
 HALF = PARTS // 2
 PROJ_PART = PROJ // PARTS
-SENDS = 5 * PARTS
+RING_PARTS = (2, 2, 2)
+RING_SENDS = 3 * PARTS + HALF + sum(RING_PARTS)
+Z_SENDS = 2 * PARTS + 2 * sum(PARTS - count for count in RING_PARTS)
+SENDS = max(RING_SENDS, Z_SENDS)
 STENCIL = (
     -5369.0 / 1800.0,
     12.0 / 7.0,
@@ -30,6 +35,8 @@
 F32, BF16 = jnp.float32, jnp.bfloat16
 MESH = pl.DeviceIdType.MESH
 REACHED = (1, 2, -1, -2)
+REACHED_BY_MATE = (0,) + REACHED
+SIDES = (1, -1)
 
 
 def split(x):
@@ -79,15 +86,19 @@
     wave_hbm, pot_hbm, proj_hbm, kb_hbm, atom_hbm, corner_hbm, out_ref,
     wave_ref, pot_ref, proj_ref, kb_fetched, atom_ref, corner_ref, fetched,
     pbuf, halo, part_own, part_in, kb_own, kb_in, fields, boxes, acc, deposit_in,
+    mate_field, mate_boxes, mate_acc, mate_part, mate_part_in,
     pick_z, pick_zt, pick_atom, pick_atom_t, band_z, cross, x_corner, local,
-    gather_out, gather_in, halo_out, halo_in_sem, part_out_sem, part_in_sem, kb_out_sem, kb_in_sem,
+    gather_out, gather_in, mate_out_sem, mate_in_sem, halo_out, halo_in_sem, part_out_sem, part_in_sem, kb_out_sem, kb_in_sem,
 ):
     dom, band = lax.axis_index("dom"), lax.axis_index("band")
     doms = lax.axis_size("dom")
     y, z = lax.rem(band, Y_RING), lax.div(band, Y_RING)
 
-    def dom_at(step):
-        return lax.rem(dom + step + doms, doms)
+    def inside(step):
+        return (dom + step >= 0) & (dom + step < doms)
+
+    def where_inside(step, work):
+        pl.when(inside(step))(work)
 
     def band_at(dy, other):
         column = 1 - z if other else z
@@ -116,7 +127,11 @@
     for target in gather_to:
         pl.semaphore_signal(barrier, inc=1, device_id=(dom, target), device_id_type=MESH)
     for step in REACHED:
-        pl.semaphore_signal(barrier, inc=1, device_id=(dom_at(step), band), device_id_type=MESH)
+
+        @functools.partial(where_inside, step)
+        def _():
+            for target in (band, gather_to[2]):
+                pl.semaphore_signal(barrier, inc=1, device_id=(dom + step, target), device_id_type=MESH)
 
     def piece(way, n, owner, part):
         ref = pbuf.at[owner, pl.ds(part * PROJ_PART, PROJ_PART)]
@@ -142,7 +157,7 @@
                 x = proj_ref[pl.ds(64 * g + p, 8, stride=8), :]
                 pbuf[band, p, :, pl.ds(128 * g, 128)] = transposed_parts(x)
         if part == 0:
-            pl.semaphore_wait(barrier, 3 + len(REACHED))
+            pl.semaphore_wait(barrier, 3 + 2 * sum(inside(step).astype(jnp.int32) for step in REACHED))
         for way in range(3):
             send(way, part, band, part)
 
@@ -151,20 +166,34 @@
         return pltpu.make_async_remote_copy(
             src_ref=source.at[planes], dst_ref=halo.at[app, side],
             send_sem=halo_out.at[app, side], recv_sem=halo_in_sem.at[app, side],
-            device_id=(dom_at(1 if side == 0 else -1), band), device_id_type=MESH,
+            device_id=(dom + (1 if side == 0 else -1), band), device_id_type=MESH,
         )
 
     def part_copy(app, n):
         return pltpu.make_async_remote_copy(
             src_ref=part_own.at[app], dst_ref=part_in.at[app, n],
             send_sem=part_out_sem.at[app, n], recv_sem=part_in_sem.at[app, n],
-            device_id=(dom_at(REACHED[n]), band), device_id_type=MESH,
+            device_id=(dom + REACHED[n], band), device_id_type=MESH,
+        )
+
+    def mate_copy():
+        return pltpu.make_async_remote_copy(
+            src_ref=wave_ref.at[pl.ds((SX // 2) * (1 - z), SX)], dst_ref=mate_field,
+            send_sem=mate_out_sem.at[0], recv_sem=mate_in_sem.at[0],
+            device_id=(dom, gather_to[2]), device_id_type=MESH,
+        )
+
+    def mate_part_copy(n):
+        return pltpu.make_async_remote_copy(
+            src_ref=mate_part, dst_ref=mate_part_in.at[n],
+            send_sem=mate_out_sem.at[1 + n], recv_sem=mate_in_sem.at[1 + n],
+            device_id=(dom + REACHED_BY_MATE[n], gather_to[2]), device_id_type=MESH,
         )
 
     def kb_copy(n):
         return pltpu.make_async_remote_copy(
             src_ref=kb_own, dst_ref=kb_in.at[n], send_sem=kb_out_sem.at[n], recv_sem=kb_in_sem.at[n],
-            device_id=(dom_at(1 if n == 0 else -1), band), device_id_type=MESH,
+            device_id=(dom + (1 if n == 0 else -1), band), device_id_type=MESH,
         )
 
     def field(app):
@@ -173,57 +202,68 @@
     for fetch in fetches[1:]:
         fetch.wait()
     kb_own[:, 0:ATOM_DEV] = kb_fetched[...]
+    mate_copy().start()
     for n in range(2):
-        kb_copy(n).start()
+        where_inside(SIDES[n], kb_copy(n).start)
     for side in range(2):
-        halo_copy(0, side, field(0)).start()
-
-    lane = iota((8, 128), 1)
-    lane_slot, lane_cell = lane >> 4, lane & 15
-    pad_rows = iota((128, 128), 0)
-    first_atom = (dom - 1) * ATOM_DEV
-    for g in range(4):
-        at_x, at_z, atom = (jnp.zeros((8, 128), jnp.int32) for _ in range(3))
-        for q in range(8):
-            here = lane_slot == q
-            at_x = jnp.where(here, corner_ref[0, 8 * g + q], at_x)
-            at_z = jnp.where(here, corner_ref[2, 8 * g + q], at_z)
-            atom = jnp.where(here, atom_ref[8 * g + q] - first_atom, atom)
-        lanes = pl.ds(128 * g, 128)
-        x_corner[:, lanes] = at_x
-        hot_z = jnp.where(pad_rows == (at_z + lane_cell)[0:1, :], F32(1.0), F32(0.0))
-        pick_z[:, lanes] = hot_z.astype(BF16)
-        pick_zt[lanes, :] = jnp.transpose(hot_z).astype(BF16)
-        hot_atom = jnp.where(pad_rows == atom[0:1, :], F32(1.0), F32(0.0))
-        pick_atom[:, lanes] = hot_atom.astype(BF16)
-        pick_atom_t[lanes, :] = jnp.transpose(hot_atom).astype(BF16)
-
-    def extract(app):
-        rows = field(app)[...].reshape(ROWS, CZ)
-        high, low = split(rows)
+        where_inside(SIDES[side], halo_copy(0, side, field(0)).start)
+
+    def make_picks():
+        lane = iota((8, 128), 1)
+        lane_slot, lane_cell = lane >> 4, lane & 15
+        pad_rows = iota((128, 128), 0)
+        first_atom = (dom - 1) * ATOM_DEV
+        for g in range(4):
+            at_x, at_z, atom = (jnp.zeros((8, 128), jnp.int32) for _ in range(3))
+            for q in range(8):
+                here = lane_slot == q
+                at_x = jnp.where(here, corner_ref[0, 8 * g + q], at_x)
+                at_z = jnp.where(here, corner_ref[2, 8 * g + q], at_z)
+                atom = jnp.where(here, atom_ref[8 * g + q] - first_atom, atom)
+            lanes = pl.ds(128 * g, 128)
+            x_corner[:, lanes] = at_x
+            hot_z = jnp.where(pad_rows == (at_z + lane_cell)[0:1, :], F32(1.0), F32(0.0))
+            pick_z[:, lanes] = hot_z.astype(BF16)
+            pick_zt[lanes, :] = jnp.transpose(hot_z).astype(BF16)
+            hot_atom = jnp.where(pad_rows == atom[0:1, :], F32(1.0), F32(0.0))
+            pick_atom[:, lanes] = hot_atom.astype(BF16)
+            pick_atom_t[lanes, :] = jnp.transpose(hot_atom).astype(BF16)
+
+    def extract(planes, out):
+        count = out.shape[0] // 2
+        extent = count + CX - SX
+        high, low = split(planes[...].reshape(extent * CY, CZ))
         for g in range(4):
             lanes = pl.ds(128 * g, 128)
             hot = pick_z[:, lanes]
-            along_z = (dot(high, hot) + dot(low, hot)).reshape(CX, CY, 128)
+            along_z = (dot(high, hot) + dot(low, hot)).reshape(extent, CY, 128)
             at_x = x_corner[:, lanes][None, 0:1, :]
-            cut = along_z[0:SX]
+            cut = along_z[0:count]
             for d in range(1, CX - SX + 1):
-                cut = jnp.where(at_x == d, along_z[d : d + SX], cut)
-            boxes[:, :, lanes] = cut.reshape(2 * SX, 8, 128)
-
-    extract(0)
-
-    distance = jnp.abs(iota((CZ, CZ), 0) - iota((CZ, CZ), 1))
-    band_z[:, 0:128], band_z[:, 128:256] = split(weight_at(distance, 3.0 * KINETIC[0]))
-    row, col = iota((ROWS, ROWS), 0), iota((ROWS, ROWS), 1)
-    gap_x, gap_y = jnp.abs((row >> 4) - (col >> 4)), jnp.abs((row & 15) - (col & 15))
-    gap = jnp.where(gap_x == 0, gap_y, jnp.where(gap_y == 0, gap_x, 99))
-    cross[0:ROWS, :], cross[ROWS:, :] = split(weight_at(gap, 0.0))
-    acc[...] = jnp.zeros((PROJ, 8, LANES), F32)
-
-    def accumulate(owner, part):
+                cut = jnp.where(at_x == d, along_z[d : d + count], cut)
+            out[:, :, lanes] = cut.reshape(2 * count, 8, 128)
+
+    def make_stencil():
+        distance = jnp.abs(iota((CZ, CZ), 0) - iota((CZ, CZ), 1))
+        band_z[:, 0:128], band_z[:, 128:256] = split(weight_at(distance, 3.0 * KINETIC[0]))
+        row, col = iota((ROWS, ROWS), 0), iota((ROWS, ROWS), 1)
+        gap_x, gap_y = jnp.abs((row >> 4) - (col >> 4)), jnp.abs((row & 15) - (col & 15))
+        gap = jnp.where(gap_x == 0, gap_y, jnp.where(gap_y == 0, gap_x, 99))
+        cross[0:ROWS, :], cross[ROWS:, :] = split(weight_at(gap, 0.0))
+
+    def accumulate(step, part, own=True, mate=True):
+        owner, at = band_at(step, False), lax.rem(y + step + Y_RING, Y_RING)
         here = pl.ds(part * PROJ_PART, PROJ_PART)
-        acc[here] = acc[here] + pbuf[owner, here] * boxes[owner][None]
+        values = pbuf[owner, here]
+        for wanted, total, cells in ((own, acc, boxes[owner]), (mate, mate_acc, mate_boxes[at])):
+            if wanted:
+                term = values * cells[None]
+                total[here] = term if step == 0 else total[here] + term
+
+    def atom_partials(total):
+        high, low = split(total[...].reshape(PROJ * 8, LANES))
+        hot = pick_atom_t[...]
+        return jnp.sum((dot(high, hot) + dot(low, hot)).reshape(PROJ, 8, 128), axis=1)
 
     def apply_local(app):
         rows = field(app)[...].reshape(ROWS, CZ)
@@ -238,7 +278,7 @@
 
     def add_halo(app):
         for side in range(2):
-            halo_copy(app, side, field(app)).wait_recv()
+            where_inside(-SIDES[side], halo_copy(app, side, field(app)).wait_recv)
         low = jnp.where(dom > 0, halo[app, 0], F32(0.0))
         high = jnp.where(dom < doms - 1, halo[app, 1], F32(0.0))
         for x in range(REACH):
@@ -246,95 +286,127 @@
             at = CX - 1 - x
             local[at] = local[at] + sum(F32(KINETIC[k]) * high[k - 1 - x] for k in range(x + 1, REACH + 1))
 
-    both_halves = tuple(range(PARTS))
-    first_half, last_half = both_halves[:HALF], both_halves[HALF:]
-
-    for part in both_halves:
-        accumulate(band, part)
-    z_next = PARTS
-    z_expected = [(band_at(0, True), part) for part in both_halves]
-    for step in range(1, 5):
-        arrived = []
-        for part in both_halves:
-            for way, sign in ((0, -1), (1, 1)):
-                if step == 4 and part not in (first_half, last_half)[way]:
-                    continue
+    all_parts = tuple(range(PARTS))
+    halves = all_parts[:HALF], all_parts[HALF:]
+    ways = ((0, -1), (1, 1))
+    z_expected = [(band_at(0, True), part) for part in all_parts]
+    z_waiting = []
+
+    def to_mate(step, part):
+        z_waiting.append((step, part))
+
+    def flush_to_mate():
+        for step, part in z_waiting:
+            send(2, len(z_expected), band_at(step, False), part)
+            z_expected.append((band_at(step, True), part))
+        z_waiting.clear()
+
+    def other_ring(hop, part):
+        return 3 * PARTS + HALF + sum(RING_PARTS[:hop]) + part
+
+    def pass_other(hop):
+        for part in range(RING_PARTS[hop - 1] if hop else RING_PARTS[0]):
+            for way, sign in ways:
+                owner = band_at(sign * hop, True)
+                if hop:
+                    received(way, other_ring(hop - 1, part), owner, part)
+                elif way == 0:
+                    received(2, part, owner, part)
+                if hop < 3 and part < RING_PARTS[hop]:
+                    send(way, other_ring(hop, part), owner, part)
+
+    for step in range(1, 4):
+        for part in all_parts:
+            for way, sign in ways:
                 owner = band_at(sign * step, False)
-                n = (step - 1) * PARTS + (part if step < 4 or way == 0 else part - HALF)
-                received(way, n, owner, part)
+                received(way, (step - 1) * PARTS + part, owner, part)
                 if step < 3:
                     send(way, step * PARTS + part, owner, part)
-                elif step == 3 and part in (first_half, last_half)[way]:
-                    send(way, 3 * PARTS + part - (0 if way == 0 else HALF), owner, part)
-                if part in last_half or step == 4:
-                    send(2, z_next, owner, part)
-                    z_expected.append((band_at(sign * step, True), part))
-                    z_next += 1
-                arrived.append((owner, part))
-        other_base = 3 * PARTS + HALF
+                elif part in halves[way]:
+                    send(way, 3 * PARTS + part - halves[way][0], owner, part)
+                if part >= RING_PARTS[step - 1]:
+                    to_mate(sign * step, part)
+                    flush_to_mate()
+        pass_other(step - 1)
         if step == 1:
-            for part in both_halves:
-                owner = band_at(0, True)
-                received(2, part, owner, part)
-                if part in first_half:
-                    for way in range(2):
-                        send(way, other_base + part, owner, part)
-                arrived.append((owner, part))
+            make_picks()
+            extract(field(0), boxes)
+            for part in all_parts:
+                accumulate(0, part, mate=False)
+                for sign in (-1, 1):
+                    accumulate(sign, part, mate=False)
+        elif step == 2:
+            mate_copy().wait_recv()
+            extract(mate_field, mate_boxes)
+            for part in all_parts:
+                accumulate(0, part, own=False)
+                for sign in (-1, 1):
+                    accumulate(sign, part, own=False)
+                    accumulate(2 * sign, part)
         else:
-            for part in first_half:
-                for way, sign in ((0, -1), (1, 1)):
-                    owner = band_at(sign * (step - 1), True)
-                    n = other_base + (step - 2) * HALF + part
-                    received(way, n, owner, part)
-                    if step < 4:
-                        send(way, n + HALF, owner, part)
-                    arrived.append((owner, part))
-        for owner, part in arrived:
-            accumulate(owner, part)
-        if step == 1:
-            apply_local(0)
-    for n in range(PARTS, SENDS):
-        owner, part = z_expected[n]
-        received(2, n, owner, part)
-        accumulate(owner, part)
+            for part in all_parts:
+                for sign in (-1, 1):
+                    accumulate(3 * sign, part)
+    for part in range(HALF):
+        for way, sign in ways:
+            at = halves[way][part]
+            received(way, 3 * PARTS + part, band_at(4, False), at)
+            to_mate(4, at)
+            flush_to_mate()
+            accumulate(4, at)
+    part_own[0] = atom_partials(acc)
+    mate_part[...] = atom_partials(mate_acc)
+    for n in range(len(REACHED)):
+        where_inside(REACHED[n], part_copy(0, n).start)
+        where_inside(REACHED[n], mate_part_copy(n + 1).start)
+    mate_part_copy(0).start()
+    pass_other(3)
+    make_stencil()
+    apply_local(0)
+    for n, (owner, part) in enumerate(z_expected):
+        if n >= PARTS or part >= RING_PARTS[0]:
+            received(2, n, owner, part)
+    add_halo(0)
 
     for n in range(2):
-        kb_copy(n).wait_recv()
+        where_inside(-SIDES[n], kb_copy(n).wait_recv)
     atom_lane = iota((8, 128), 1)
     energy = jnp.where(
         atom_lane < ATOM_DEV,
-        kb_in[0],
+        jnp.where(dom > 0, kb_in[0], F32(0.0)),
         jnp.where(
             atom_lane < 2 * ATOM_DEV,
             pltpu.roll(kb_own[...], ATOM_DEV, 1),
-            jnp.where(atom_lane < 3 * ATOM_DEV, pltpu.roll(kb_in[1], 2 * ATOM_DEV, 1), F32(0.0)),
+            jnp.where((atom_lane < 3 * ATOM_DEV) & (dom < doms - 1), pltpu.roll(kb_in[1], 2 * ATOM_DEV, 1), F32(0.0)),
         ),
     )
     centre, coefs = coefficients()
     for app in range(DEGREE):
         if app:
-            extract(app)
+            extract(field(app), boxes)
             for g in range(4):
                 lanes = pl.ds(128 * g, 128)
                 total = pbuf[0, :, :, lanes] * boxes[0, :, lanes][None]
                 for owner in range(1, 2 * SX):
                     total = total + pbuf[owner, :, :, lanes] * boxes[owner, :, lanes][None]
                 acc[:, :, lanes] = total
-        high, low = split(acc[...].reshape(PROJ * 8, LANES))
-        hot = pick_atom_t[...]
-        sums = (dot(high, hot) + dot(low, hot)).reshape(PROJ, 8, 128)
-        part_own[app] = jnp.sum(sums, axis=1)
-        for n in range(len(REACHED)):
-            part_copy(app, n).start()
-        if app:
+            part_own[app] = atom_partials(acc)
+            for n in range(len(REACHED)):
+                where_inside(REACHED[n], part_copy(app, n).start)
             apply_local(app)
-        add_halo(app)
+            add_halo(app)
         total = part_own[app]
+        if app == 0:
+            mate_part_copy(0).wait_recv()
+            total = total + mate_part_in[0]
         for n, step in enumerate(REACHED):
-            part_copy(app, n).wait_recv()
-            inside = (dom - step >= 0) & (dom - step < doms)
-            shifted = pltpu.roll(part_in[app, n], (-step * ATOM_DEV) % 128, 1)
-            total = total + jnp.where(inside, shifted, F32(0.0))
+            where_inside(-step, part_copy(app, n).wait_recv)
+            partial = part_in[app, n]
+            if app == 0:
+                where_inside(-step, mate_part_copy(n + 1).wait_recv)
+                partial = partial + mate_part_in[n + 1]
+            shifted = pltpu.roll(partial, (-step * ATOM_DEV) % 128, 1)
+            total = total + jnp.where(inside(-step), shifted, F32(0.0))
         high, low = split(total * energy)
         for g in range(4):
             lanes = pl.ds(128 * g, 128)
@@ -365,19 +437,22 @@
         if app < DEGREE - 1:
             fields[app] = new
             for side in range(2):
-                halo_copy(app + 1, side, field(app + 1)).start()
+                where_inside(SIDES[side], halo_copy(app + 1, side, field(app + 1)).start)
         else:
             out_ref[0] = new
 
     for copy in sent:
         copy.wait_send()
+    mate_copy().wait_send()
+    for n in range(len(REACHED_BY_MATE)):
+        where_inside(REACHED_BY_MATE[n], mate_part_copy(n).wait_send)
     for n in range(2):
-        kb_copy(n).wait_send()
+        where_inside(SIDES[n], kb_copy(n).wait_send)
     for app in range(DEGREE):
         for side in range(2):
-            halo_copy(app, side, field(app)).wait_send()
+            where_inside(SIDES[side], halo_copy(app, side, field(app)).wait_send)
         for n in range(len(REACHED)):
-            part_copy(app, n).wait_send()
+            where_inside(REACHED[n], part_copy(app, n).wait_send)
 
 
 def on_device(wave_block, potential, projectors, kb_energy, slot_atom, slot_corner):
@@ -406,6 +481,11 @@
             pltpu.VMEM((2 * SX, 8, LANES), F32),
             pltpu.VMEM((PROJ, 8, LANES), F32),
             pltpu.VMEM((ROWS, LANES), F32),
+            pltpu.VMEM((SX, CY, CZ), F32),
+            pltpu.VMEM((SX, 8, LANES), F32),
+            pltpu.VMEM((PROJ, 8, LANES), F32),
+            pltpu.VMEM((8, 128), F32),
+            pltpu.VMEM((len(REACHED_BY_MATE), 8, 128), F32),
             pltpu.VMEM((CZ, LANES), BF16),
             pltpu.VMEM((LANES, CZ), BF16),
             pltpu.VMEM((128, LANES), BF16),
@@ -416,6 +496,8 @@
             pltpu.VMEM((CX, CY, CZ), F32),
             dma((3, SENDS)),
             dma((3, SENDS)),
+            dma((1 + len(REACHED_BY_MATE),)),
+            dma((1 + len(REACHED_BY_MATE),)),
             dma((DEGREE, 2)),
             dma((DEGREE, 2)),
             dma((DEGREE, len(REACHED))),

time: 54.8 us -> 48.2 us (0.88)
  Pallas kernels: 53.1 us -> 46.2 us
    pallas_call x1, Pallas kernels: 53.1 us -> 46.2 us  [on_device(): pl.pallas_call(kernel, out_shape=jax.ShapeDtypeStruct(wave_block.shape, F...]
where the time goes in v2:
time: 48.2 us; the launch traced here: 47.8 us
  Pallas kernels  46.2 us (96%)
  local copies, waits for them, and re-layouts  1.54 us (3%)
    pallas_call x1, Pallas kernels, on_device(): pl.pallas_call(kernel, out_shape=jax.ShapeDtypeStruct(wave_block.shape, F...  46.2 us
    unnamed x1, local copies, waits for them, and re-layouts  1.54 us

profile of v2, /device:TPU:1, one launch (start us, length us, event | category | flops | bytes accessed | tf_op | source)
XLA Modules:
  0.0 47.8 jit_solution(17868584363360261994)
XLA Ops:
  0.0 46.2 %chebyshev.1 = f32[1,12,16,128]{3,2,1,0:T(8,128)} custom-call(f32[1,12,16,128]{3,2,1,0:T(8,128)} %wave_hbm.1, f32[12,16,128]{2,1,0:T(8,128)} %pot_hbm.1, f32[256,128]{1,0:T(8,128)} %bitcast.2, f32[8,16]{1,0:T(8,128)} %bitcast.3, s32[32]{0:T(128)} %atom_hbm.1, s32[3,32]{1,0:T(4,128)} %corner_hbm.1), custom_call_target="tpu_custom_call" | custom-call | tf_op jit(solution)/shard_map/chebyshev/pallas_call | solution.py:461
  46.3 1.5 %copy.8 = f32[1,12,16,128]{3,2,1,0:T(8,128)} copy(f32[1,12,16,128]{3,2,1,0:T(8,128)} %chebyshev.1) | data formatting | bytes 196608

commit v3 on v2

--- a/solution.py
+++ b/solution.py
@@ -44,6 +44,17 @@
     return high, (x - high.astype(F32)).astype(BF16)
 
 
+def halves_beside(x):
+    return jnp.concatenate(split(x), axis=1)
+
+
+def dot_below(x, table):
+    rows = x.shape[0]
+    high = x.astype(BF16).astype(F32)
+    both = dot(jnp.concatenate([high, x - high], axis=0).astype(BF16), table)
+    return both[0:rows] + both[rows:]
+
+
 def dot(a, b):
     return jnp.dot(a, b, preferred_element_type=F32)
 
@@ -105,6 +116,16 @@
         return column * Y_RING + lax.rem(y + dy + Y_RING, Y_RING)
 
     gather_to = (band_at(1, False), band_at(-1, False), band_at(0, True))
+
+    barrier = pltpu.get_barrier_semaphore()
+    for target in gather_to:
+        pl.semaphore_signal(barrier, inc=1, device_id=(dom, target), device_id_type=MESH)
+    for step in REACHED:
+
+        @functools.partial(where_inside, step)
+        def _():
+            for target in (band, gather_to[2]):
+                pl.semaphore_signal(barrier, inc=1, device_id=(dom + step, target), device_id_type=MESH)
 
     kb_own[...] = jnp.zeros((8, 128), F32)
     fetches = [
@@ -122,16 +143,6 @@
     ]
     for fetch in fetches:
         fetch.start()
-
-    barrier = pltpu.get_barrier_semaphore()
-    for target in gather_to:
-        pl.semaphore_signal(barrier, inc=1, device_id=(dom, target), device_id_type=MESH)
-    for step in REACHED:
-
-        @functools.partial(where_inside, step)
-        def _():
-            for target in (band, gather_to[2]):
-                pl.semaphore_signal(barrier, inc=1, device_id=(dom + step, target), device_id_type=MESH)
 
     def piece(way, n, owner, part):
         ref = pbuf.at[owner, pl.ds(part * PROJ_PART, PROJ_PART)]
@@ -223,7 +234,7 @@
             lanes = pl.ds(128 * g, 128)
             x_corner[:, lanes] = at_x
             hot_z = jnp.where(pad_rows == (at_z + lane_cell)[0:1, :], F32(1.0), F32(0.0))
-            pick_z[:, lanes] = hot_z.astype(BF16)
+            pick_z[0:CZ, lanes] = pick_z[CZ:, lanes] = hot_z.astype(BF16)
             pick_zt[lanes, :] = jnp.transpose(hot_z).astype(BF16)
             hot_atom = jnp.where(pad_rows == atom[0:1, :], F32(1.0), F32(0.0))
             pick_atom[:, lanes] = hot_atom.astype(BF16)
@@ -232,11 +243,10 @@
     def extract(planes, out):
         count = out.shape[0] // 2
         extent = count + CX - SX
-        high, low = split(planes[...].reshape(extent * CY, CZ))
+        rows = halves_beside(planes[...].reshape(extent * CY, CZ))
         for g in range(4):
             lanes = pl.ds(128 * g, 128)
-            hot = pick_z[:, lanes]
-            along_z = (dot(high, hot) + dot(low, hot)).reshape(extent, CY, 128)
+            along_z = dot(rows, pick_z[:, lanes]).reshape(extent, CY, 128)
             at_x = x_corner[:, lanes][None, 0:1, :]
             cut = along_z[0:count]
             for d in range(1, CX - SX + 1):
@@ -261,9 +271,8 @@
                 total[here] = term if step == 0 else total[here] + term
 
     def atom_partials(total):
-        high, low = split(total[...].reshape(PROJ * 8, LANES))
-        hot = pick_atom_t[...]
-        return jnp.sum((dot(high, hot) + dot(low, hot)).reshape(PROJ, 8, 128), axis=1)
+        by_slot = jnp.sum(total[...], axis=1)
+        return dot_below(by_slot, pick_atom_t[...])
 
     def apply_local(app):
         rows = field(app)[...].reshape(ROWS, CZ)
@@ -302,17 +311,17 @@
         z_waiting.clear()
 
     def other_ring(hop, part):
-        return 3 * PARTS + HALF + sum(RING_PARTS[:hop]) + part
+        return 3 * PARTS + HALF + sum(RING_PARTS[: hop + 1]) + part - PARTS
 
     def pass_other(hop):
-        for part in range(RING_PARTS[hop - 1] if hop else RING_PARTS[0]):
+        for part in range(PARTS - RING_PARTS[max(hop - 1, 0)], PARTS):
             for way, sign in ways:
                 owner = band_at(sign * hop, True)
                 if hop:
                     received(way, other_ring(hop - 1, part), owner, part)
                 elif way == 0:
                     received(2, part, owner, part)
-                if hop < 3 and part < RING_PARTS[hop]:
+                if hop < 3 and part >= PARTS - RING_PARTS[hop]:
                     send(way, other_ring(hop, part), owner, part)
 
     for step in range(1, 4):
@@ -324,7 +333,7 @@
                     send(way, step * PARTS + part, owner, part)
                 elif part in halves[way]:
                     send(way, 3 * PARTS + part - halves[way][0], owner, part)
-                if part >= RING_PARTS[step - 1]:
+                if part < PARTS - RING_PARTS[step - 1]:
                     to_mate(sign * step, part)
                     flush_to_mate()
         pass_other(step - 1)
@@ -364,7 +373,7 @@
     make_stencil()
     apply_local(0)
     for n, (owner, part) in enumerate(z_expected):
-        if n >= PARTS or part >= RING_PARTS[0]:
+        if n >= PARTS or part < PARTS - RING_PARTS[0]:
             received(2, n, owner, part)
     add_halo(0)
 
@@ -407,11 +416,10 @@
                 partial = partial + mate_part_in[n + 1]
             shifted = pltpu.roll(partial, (-step * ATOM_DEV) % 128, 1)
             total = total + jnp.where(inside(-step), shifted, F32(0.0))
-        high, low = split(total * energy)
+        back_all = dot_below(total * energy, pick_atom[...])
         for g in range(4):
             lanes = pl.ds(128 * g, 128)
-            hot = pick_atom[:, lanes]
-            back = dot(high, hot) + dot(low, hot)
+            back = back_all[:, 128 * g : 128 * (g + 1)]
             weights = [jnp.broadcast_to(back[p : p + 1, :], (8, 128)) for p in range(PROJ)]
             at_x = x_corner[:, lanes]
             for half in range(2):
@@ -426,9 +434,7 @@
                     for d in range(max(0, x - SX + 1), min(x, CX - SX) + 1):
                         spread = jnp.where(at_x == d, values[x - d], spread)
                     deposit_in[pl.ds(x * CY + 8 * half, 8), lanes] = spread
-        high, low = split(deposit_in[...])
-        hot = pick_zt[...]
-        nonlocal_part = (dot(high, hot) + dot(low, hot)).reshape(CX, CY, CZ)
+        nonlocal_part = dot_below(deposit_in[...], pick_zt[...]).reshape(CX, CY, CZ)
         now = field(app)[...]
         scale, keep = coefs[app]
         new = F32(scale) * (local[...] + nonlocal_part - F32(centre) * now)
@@ -486,7 +492,7 @@
             pltpu.VMEM((PROJ, 8, LANES), F32),
             pltpu.VMEM((8, 128), F32),
             pltpu.VMEM((len(REACHED_BY_MATE), 8, 128), F32),
-            pltpu.VMEM((CZ, LANES), BF16),
+            pltpu.VMEM((2 * CZ, LANES), BF16),
             pltpu.VMEM((LANES, CZ), BF16),
             pltpu.VMEM((128, LANES), BF16),
             pltpu.VMEM((LANES, 128), BF16),
@@ -506,7 +512,7 @@
             dma((2,)),
         ],
         compiler_params=pltpu.CompilerParams(
-            collective_id=0, has_side_effects=True, vmem_limit_bytes=60 * 1024 * 1024
+            collective_id=0, has_side_effects=True, vmem_limit_bytes=56 * 1024 * 1024
         ),
         name="chebyshev",
     )(wave_block, potential, projectors.reshape(SLOTS * PROJ, 128), kb_energy.T, slot_atom, slot_corner)

time: 48.2 us -> 47.7 us (0.990)
  Pallas kernels: 46.2 us -> 45.4 us
    pallas_call x1, Pallas kernels: 46.2 us -> 45.4 us  [on_device(): pl.pallas_call(kernel, out_shape=jax.ShapeDtypeStruct(wave_block.shape, F...]
where the time goes in v3:
time: 47.7 us; the launch traced here: 47 us
  Pallas kernels  45.4 us (95%)
  local copies, waits for them, and re-layouts  1.54 us (3%)
    pallas_call x1, Pallas kernels, on_device(): pl.pallas_call(kernel, out_shape=jax.ShapeDtypeStruct(wave_block.shape, F...  45.4 us
    unnamed x1, local copies, waits for them, and re-layouts  1.54 us

profile of v3, /device:TPU:1, one launch (start us, length us, event | category | flops | bytes accessed | tf_op | source)
XLA Modules:
  0.0 47.0 jit_solution(17035352219702187918)
XLA Ops:
  0.0 45.4 %chebyshev.1 = f32[1,12,16,128]{3,2,1,0:T(8,128)} custom-call(f32[1,12,16,128]{3,2,1,0:T(8,128)} %wave_hbm.1, f32[12,16,128]{2,1,0:T(8,128)} %pot_hbm.1, f32[256,128]{1,0:T(8,128)} %bitcast.2, f32[8,16]{1,0:T(8,128)} %bitcast.3, s32[32]{0:T(128)} %atom_hbm.1, s32[3,32]{1,0:T(4,128)} %corner_hbm.1), custom_call_target="tpu_custom_call" | custom-call | tf_op jit(solution)/shard_map/chebyshev/pallas_call | solution.py:467
  45.4 1.5 %copy.8 = f32[1,12,16,128]{3,2,1,0:T(8,128)} copy(f32[1,12,16,128]{3,2,1,0:T(8,128)} %chebyshev.1) | data formatting | bytes 196608

commit v4 on v3

--- a/solution.py
+++ b/solution.py
@@ -132,7 +132,7 @@
         pltpu.make_async_copy(source, target, fetched.at[n])
         for n, (source, target) in enumerate(
             (
-                (proj_hbm, proj_ref),
+                (proj_hbm, proj_ref.at[pl.ds(0, SLOTS * PROJ)]),
                 (wave_hbm.at[0], wave_ref),
                 (corner_hbm, corner_ref),
                 (atom_hbm, atom_ref),
@@ -169,7 +169,7 @@
                 pbuf[band, p, :, pl.ds(128 * g, 128)] = transposed_parts(x)
         if part == 0:
             pl.semaphore_wait(barrier, 3 + 2 * sum(inside(step).astype(jnp.int32) for step in REACHED))
-        for way in range(3):
+        for way in (2, 0, 1):
             send(way, part, band, part)
 
     def halo_copy(app, side, source):
@@ -363,12 +363,13 @@
             to_mate(4, at)
             flush_to_mate()
             accumulate(4, at)
-    part_own[0] = atom_partials(acc)
     mate_part[...] = atom_partials(mate_acc)
     for n in range(len(REACHED)):
-        where_inside(REACHED[n], part_copy(0, n).start)
         where_inside(REACHED[n], mate_part_copy(n + 1).start)
     mate_part_copy(0).start()
+    part_own[0] = atom_partials(acc)
+    for n in range(len(REACHED)):
+        where_inside(REACHED[n], part_copy(0, n).start)
     pass_other(3)
     make_stencil()
     apply_local(0)
@@ -389,6 +390,20 @@
             jnp.where((atom_lane < 3 * ATOM_DEV) & (dom < doms - 1), pltpu.roll(kb_in[1], 2 * ATOM_DEV, 1), F32(0.0)),
         ),
     )
+    def all_left(app):
+        if app == 0:
+            for copy in sent:
+                copy.wait_send()
+            mate_copy().wait_send()
+            for n in range(len(REACHED_BY_MATE)):
+                where_inside(REACHED_BY_MATE[n], mate_part_copy(n).wait_send)
+            for n in range(2):
+                where_inside(SIDES[n], kb_copy(n).wait_send)
+        for side in range(2):
+            where_inside(SIDES[side], halo_copy(app, side, field(app)).wait_send)
+        for n in range(len(REACHED)):
+            where_inside(REACHED[n], part_copy(app, n).wait_send)
+
     centre, coefs = coefficients()
     for app in range(DEGREE):
         if app:
@@ -403,6 +418,7 @@
             for n in range(len(REACHED)):
                 where_inside(REACHED[n], part_copy(app, n).start)
             apply_local(app)
+            all_left(app - 1)
             add_halo(app)
         total = part_own[app]
         if app == 0:
@@ -447,18 +463,7 @@
         else:
             out_ref[0] = new
 
-    for copy in sent:
-        copy.wait_send()
-    mate_copy().wait_send()
-    for n in range(len(REACHED_BY_MATE)):
-        where_inside(REACHED_BY_MATE[n], mate_part_copy(n).wait_send)
-    for n in range(2):
-        where_inside(SIDES[n], kb_copy(n).wait_send)
-    for app in range(DEGREE):
-        for side in range(2):
-            where_inside(SIDES[side], halo_copy(app, side, field(app)).wait_send)
-        for n in range(len(REACHED)):
-            where_inside(REACHED[n], part_copy(app, n).wait_send)
+    all_left(DEGREE - 1)
 
 
 def on_device(wave_block, potential, projectors, kb_energy, slot_atom, slot_corner):
@@ -472,7 +477,7 @@
         scratch_shapes=[
             pltpu.VMEM((CX, CY, CZ), F32),
             pltpu.VMEM((CX, CY, CZ), F32),
-            pltpu.VMEM((SLOTS * PROJ, 128), F32),
+            pltpu.VMEM((SLOTS * PROJ + 8, 128), F32),
             pltpu.VMEM((8, ATOM_DEV), F32),
             pltpu.SMEM((SLOTS,), jnp.int32),
             pltpu.SMEM((3, SLOTS), jnp.int32),

time: 47.7 us -> 47.7 us (level)
  no operation moved by 1% of the time
where the time goes in v4:
time: 47.7 us; the launch traced here: 46.9 us
  Pallas kernels  45.4 us (95%)
  local copies, waits for them, and re-layouts  1.54 us (3%)
    pallas_call x1, Pallas kernels, on_device(): pl.pallas_call(kernel, out_shape=jax.ShapeDtypeStruct(wave_block.shape, F...  45.4 us
    unnamed x1, local copies, waits for them, and re-layouts  1.54 us

profile of v4, /device:TPU:1, one launch (start us, length us, event | category | flops | bytes accessed | tf_op | source)
XLA Modules:
  0.0 46.9 jit_solution(12293037500104632820)
XLA Ops:
  0.0 45.4 %chebyshev.1 = f32[1,12,16,128]{3,2,1,0:T(8,128)} custom-call(f32[1,12,16,128]{3,2,1,0:T(8,128)} %wave_hbm.1, f32[12,16,128]{2,1,0:T(8,128)} %pot_hbm.1, f32[256,128]{1,0:T(8,128)} %bitcast.2, f32[8,16]{1,0:T(8,128)} %bitcast.3, s32[32]{0:T(128)} %atom_hbm.1, s32[3,32]{1,0:T(4,128)} %corner_hbm.1), custom_call_target="tpu_custom_call" | custom-call | tf_op jit(solution)/shard_map/chebyshev/pallas_call | solution.py:472
  45.4 1.5 %copy.8 = f32[1,12,16,128]{3,2,1,0:T(8,128)} copy(f32[1,12,16,128]{3,2,1,0:T(8,128)} %chebyshev.1) | data formatting | bytes 196608

commit v5 on v4

--- a/solution.py
+++ b/solution.py
@@ -417,6 +417,8 @@
             part_own[app] = atom_partials(acc)
             for n in range(len(REACHED)):
                 where_inside(REACHED[n], part_copy(app, n).start)
+            for side in range(2):
+                where_inside(SIDES[side], halo_copy(app, side, field(app)).start)
             apply_local(app)
             all_left(app - 1)
             add_halo(app)
@@ -458,8 +460,6 @@
             new = new - F32(keep) * field(app - 1)[...]
         if app < DEGREE - 1:
             fields[app] = new
-            for side in range(2):
-                where_inside(SIDES[side], halo_copy(app + 1, side, field(app + 1)).start)
         else:
             out_ref[0] = new
 

time: 47.7 us -> 48.6 us (1.019)
  the two profiles are of different devices: /device:TPU:1 before, /device:TPU:10 now
where the time goes in v5:
time: 48.6 us; the launch traced here: 48.4 us
  Pallas kernels  46.9 us (97%)
  local copies, waits for them, and re-layouts  1.54 us (3%)
    pallas_call x1, Pallas kernels, on_device(): pl.pallas_call(kernel, out_shape=jax.ShapeDtypeStruct(wave_block.shape, F...  46.9 us
    unnamed x1, local copies, waits for them, and re-layouts  1.54 us

profile of v5, /device:TPU:10, one launch (start us, length us, event | category | flops | bytes accessed | tf_op | source)
XLA Modules:
  0.0 48.4 jit_solution(6931771613316634338)
XLA Ops:
  0.0 46.9 %chebyshev.1 = f32[1,12,16,128]{3,2,1,0:T(8,128)} custom-call(f32[1,12,16,128]{3,2,1,0:T(8,128)} %wave_hbm.1, f32[12,16,128]{2,1,0:T(8,128)} %pot_hbm.1, f32[256,128]{1,0:T(8,128)} %bitcast.2, f32[8,16]{1,0:T(8,128)} %bitcast.3, s32[32]{0:T(128)} %atom_hbm.1, s32[3,32]{1,0:T(4,128)} %corner_hbm.1), custom_call_target="tpu_custom_call" | custom-call | tf_op jit(solution)/shard_map/chebyshev/pallas_call | solution.py:472
  46.9 1.5 %copy.8 = f32[1,12,16,128]{3,2,1,0:T(8,128)} copy(f32[1,12,16,128]{3,2,1,0:T(8,128)} %chebyshev.1) | data formatting | bytes 196608
